TPU v7x, 512 devices: a whole 4x8x8 slice. The times are simulated.
512 devices in a mesh: seq: 128 (over z, y_hi, x), chan: 4 (over y_lo, core).
Axes of the slice: x: 4, y: 8 (y_hi: 4, y_lo: 2; y = y_hi * 2 + y_lo), z: 8, core: 2. Of those that a mesh axis runs over, the one named last changes fastest.
Arguments:
- inputs: bfloat16 [262144, 512], P('seq', 'chan'), may hold values from -6 to 6
- gate: bfloat16 [262144, 512], P('seq', 'chan'), may hold values from -6 to 6
- cotangent: bfloat16 [262144, 512], P('seq', 'chan'), may hold values from -1.1953125 to 1.1953125
- right_factor: bfloat16 [512, 512, 512], P('seq', 'chan'), may hold values from -0.25 to 0.25
- left_factor: bfloat16 [512, 512, 512], P('seq', 'chan'), may hold values from -0.25 to 0.25
Outputs:
- input_grad: bfloat16 [262144, 512], P('seq', 'chan')
- gate_grad: bfloat16 [262144, 512], P('seq', 'chan')
- right_grad: bfloat16 [512, 512, 512], P('seq', 'chan')
- left_grad: bfloat16 [512, 512, 512], P('seq', 'chan')
All inputs are finite; a program needn't handle non-finite values.
Results may differ from a plain program's by a relative error of at most 0.013.
Values may be sent and summed in bfloat16 or wider, within the bound.
A program may use at most 64 MiB of HBM per device.

v0:
```python
import jax
import jax.numpy as jnp
from jax import lax
from jax.sharding import PartitionSpec as P


def shards(inputs, gate, cotangent, right_factor, left_factor):
    blocks = right_factor.shape[0]
    order = right_factor.shape[2]
    chans = inputs.shape[1]
    grid_in = inputs.reshape(blocks, order, chans)
    gate_rows = gate.reshape(blocks, order, chans)
    cot_rows = cotangent.reshape(blocks, order, chans)
    upper = jnp.einsum(
        "bkj,bjc->bkc",
        lax.all_gather(right_factor, "chan", axis=1, tiled=True),
        grid_in,
        preferred_element_type=jnp.float32,
    )
    upper = upper.astype(jnp.bfloat16)
    upper_cols = lax.all_to_all(upper, "seq", split_axis=1, concat_axis=0, tiled=True)
    mixed = jnp.einsum(
        "kmi,ikc->mkc",
        lax.all_gather(left_factor, "chan", axis=1, tiled=True),
        upper_cols,
        preferred_element_type=jnp.float32,
    )
    mixed = mixed.astype(jnp.bfloat16)
    mixed_rows = lax.all_to_all(mixed, "seq", split_axis=0, concat_axis=1, tiled=True)
    cot_wide = cot_rows.astype(jnp.float32)
    gate_grad = (cot_wide * mixed_rows.astype(jnp.float32)).astype(jnp.bfloat16)
    back_rows = (cot_wide * gate_rows.astype(jnp.float32)).astype(jnp.bfloat16)
    back = lax.all_to_all(back_rows, "seq", split_axis=1, concat_axis=0, tiled=True)
    rows_used = back
    lower_cols = jnp.einsum(
        "kmi,mkc->ikc",
        lax.all_gather(left_factor, "chan", axis=1, tiled=True),
        rows_used,
        preferred_element_type=jnp.float32,
    )
    lower_cols = lower_cols.astype(jnp.bfloat16)
    left_terms = jnp.einsum("mkc,ikc->kmi", back, upper_cols, preferred_element_type=jnp.float32)
    left_grad = lax.psum_scatter(
        left_terms.astype(jnp.bfloat16), "chan", scatter_dimension=1, tiled=True
    )
    lower = lax.all_to_all(lower_cols, "seq", split_axis=0, concat_axis=1, tiled=True)
    rows_used = lower
    input_grad = jnp.einsum(
        "bkj,bkc->bjc",
        lax.all_gather(right_factor, "chan", axis=1, tiled=True),
        rows_used,
        preferred_element_type=jnp.float32,
    )
    input_grad = input_grad.astype(jnp.bfloat16)
    right_terms = jnp.einsum("bkc,bjc->bkj", lower, grid_in, preferred_element_type=jnp.float32)
    right_grad = lax.psum_scatter(
        right_terms.astype(jnp.bfloat16), "chan", scatter_dimension=1, tiled=True
    )
    return (
        input_grad.reshape(blocks * order, chans),
        gate_grad.reshape(blocks * order, chans),
        right_grad,
        left_grad,
    )


def solution(mesh):
    placed = (
        P("seq", "chan"),
        P("seq", "chan"),
        P("seq", "chan"),
        P("seq", "chan", None),
        P("seq", "chan", None),
    )
    return jax.shard_map(
        shards,
        mesh=mesh,
        in_specs=placed,
        out_specs=(
            P("seq", "chan"),
            P("seq", "chan"),
            P("seq", "chan", None),
            P("seq", "chan", None),
        ),
        check_vma=False,
    )
```

profile of v0, /device:TPU:1, one launch (start us, length us, event | category | flops | bytes accessed | tf_op | source)
XLA Modules:
  0.0 254.0 jit_solution(12478052317162000033)
XLA Ops:
  7.2 0.7 all-gather.5.cloned.1.call-update
  8.0 0.7 all-gather.3.cloned.1.call-update
  8.7 41.8 %all-gather.5.cloned.1.call-done = bf16[4,512,512]{2,1,0:T(8,128)(2,1)} async-done(((bf16[4,128,512]{2,1,0:T(8,128)(2,1)}), bf16[4,512,512]{2,1,0:T(8,128)(2,1)}) %all-gather.5.cloned.1.call-update) | async-done | bytes 2097168 | tf_op jit(solution)/shard_map/all_gather | solution.py:50
  50.5 2.3 convolution_convert_fusion.3
  52.8 0.4 copy.43
  53.2 41.9 %all_to_all.63 = bf16[4,512,128]{2,0,1:T(4,128)(2,1)S(1)} all-to-all(bf16[4,512,128]{2,0,1:T(4,128)(2,1)S(1)} %copy.43), channel_id=1, replica_groups=mesh['seq'=128,'chan'=4] {'seq'}, dimensions={1} | all-to-all | bytes 1048576 | tf_op jit(solution)/shard_map/all_to_all | solution.py:21
  95.1 0.2 copy.44
  95.3 3.4 %all-gather.3.cloned.1.call-done = bf16[4,512,512]{2,1,0:T(8,128)(2,1)} async-done(((bf16[4,128,512]{2,1,0:T(8,128)(2,1)}), bf16[4,512,512]{2,1,0:T(8,128)(2,1)}) %all-gather.3.cloned.1.call-update) | async-done | bytes 2097168 | tf_op jit(solution)/shard_map/all_gather | solution.py:37
  98.7 2.4 fusion.2
  101.1 0.3 copy.46
  101.5 33.6 %all_to_all.64 = bf16[512,4,128]{2,1,0:T(4,128)(2,1)S(1)} all-to-all(bf16[512,4,128]{2,1,0:T(4,128)(2,1)S(1)} %copy.46), channel_id=1, replica_groups=mesh['seq'=128,'chan'=4] {'seq'}, dimensions={0} | all-to-all | bytes 1048576 | tf_op jit(solution)/shard_map/all_to_all | solution.py:29
  135.1 0.1 copy.47
  135.2 0.1 convert_bitcast_fusion
  135.3 0.7 copy.48
  136.0 0.3 copy-done.5
  136.2 0.2 copy-done.6
  136.4 1.0 fusion.4
  137.4 0.4 copy.34
  137.8 26.9 %all_to_all.65 = bf16[4,512,128]{2,0,1:T(4,128)(2,1)S(1)} all-to-all(bf16[4,512,128]{2,0,1:T(4,128)(2,1)S(1)} %copy.34), channel_id=1, replica_groups=mesh['seq'=128,'chan'=4] {'seq'}, dimensions={1} | all-to-all | bytes 1048576 | tf_op jit(solution)/shard_map/all_to_all | solution.py:33
  164.7 0.1 copy.35
  164.8 0.4 copy.36
  165.2 0.8 copy-done.2
  166.0 2.1 convolution_convert_fusion
  168.1 1.0 copy-done.3
  169.1 1.3 fusion
  170.4 1.4 copy.38
  171.7 37.3 %all_to_all.66 = bf16[512,4,128]{2,1,0:T(4,128)(2,1)S(1)} all-to-all(bf16[512,4,128]{2,1,0:T(4,128)(2,1)S(1)} %copy.38), channel_id=1, replica_groups=mesh['seq'=128,'chan'=4] {'seq'}, dimensions={0} | all-to-all | bytes 1048576 | tf_op jit(solution)/shard_map/all_to_all | solution.py:46
  209.1 0.4 copy.40
  209.5 2.0 convolution_convert_fusion.1
  211.6 1.3 fusion.1
  212.9 2.0 copy.42
  214.9 32.6 %reduce-scatter.3.cloned.1.call-done = bf16[4,128,512]{2,1,0:T(8,128)(2,1)} async-done(((bf16[4,512,512]{2,1,0:T(8,128)(2,1)}), bf16[4,128,512]{2,1,0:T(8,128)(2,1)}) %reduce-scatter.3.cloned.1.call-update) | async-done | bytes 524304 | tf_op jit(solution)/shard_map/reduce_scatter | solution.py:56
  (18 shorter events, 0.3 us)
Async XLA Ops:
  7.2 43.4 %copy-start = (bf16[2048,128]{1,0:T(8,128)(2,1)S(1)}, bf16[2048,128]{1,0:T(8,128)(2,1)}, u32[]{:S(2)}) copy-start(bf16[2048,128]{1,0:T(8,128)(2,1)} %param.5) | copy-start | bytes 1572868
  7.2 43.3 %all-gather.5.cloned.1.call-start = ((), (), s32[]{:S(2)}) async-start(), calls=%async_computation.7 | async-start | bytes 2621440 | tf_op jit(solution)/shard_map/all_gather | solution.py:50
  7.9 90.8 %all-gather.3.cloned.1.call-start = ((), (), s32[]{:S(2)}) async-start(), calls=%async_computation.6 | async-start | bytes 2621440 | tf_op jit(solution)/shard_map/all_gather | solution.py:37
  8.7 206.3 %reduce-scatter.5.cloned.1.call-start = ((), (), s32[]{:S(2)}) async-start(), calls=%async_computation.9 | async-start | bytes 2621440 | tf_op jit(solution)/shard_map/reduce_scatter | solution.py:43
  135.2 1.0 copy-start.5
  135.2 1.2 copy-start.6
  165.2 0.8 copy-start.2
  166.0 2.1 copy-start.1
  168.0 1.0 copy-start.3
  168.1 79.4 %reduce-scatter.3.cloned.1.call-start = ((), (), s32[]{:S(2)}) async-start(), calls=%async_computation.8 | async-start | bytes 2621440 | tf_op jit(solution)/shard_map/reduce_scatter | solution.py:56
  209.5 2.1 copy-start.4
Sparse Core Ops, SparseCore 0:
  10.1 40.3 all-gather.4
  52.6 46.0 all-gather.2
  168.2 41.8 reduce-scatter.4
  213.6 33.8 reduce-scatter.2
where the time goes:
time: 254 us
  blocking collectives  140 us (55%)
  waiting for transfers between devices  79.2 us (31%)
  between operations  13.9 us (5%)
  matrix products  11.4 us (4%)
  local copies, waits for them, and re-layouts  8.59 us (3%)
    all_to_all x1, blocking collectives, shards(): lax.all_to_all(upper, 'seq', split_axis=1, concat_axis=0, tiled=True)  41.9 us
    all_gather x1, waiting for transfers between devices, shards(): lax.all_gather(right_factor, 'chan', axis=1, tiled=True)  41.8 us
    all_to_all x1, blocking collectives, shards(): lax.all_to_all(lower_cols, 'seq', split_axis=0, concat_axis=1, tiled=True)  37.3 us
    all_to_all x1, blocking collectives, shards(): lax.all_to_all(mixed, 'seq', split_axis=0, concat_axis=1, tiled=True)  33.6 us
    reduce_scatter x1, waiting for transfers between devices, shards(): lax.psum_scatter(right_terms.astype(jnp.bfloat16), 'chan', scatter_dimens...  32.6 us
    all_to_all x1, blocking collectives, shards(): lax.all_to_all(back_rows, 'seq', split_axis=1, concat_axis=0, tiled=True)  26.9 us
  transfers between devices with their start and end apart: 4, of which 3 were waited for; matrix products, arithmetic and copies ran while one was open for 4% of the time, Pallas kernels for 0%

commit v1 on v0

v1 whole, which is shorter than its diff:
```python
import functools

import jax
import jax.numpy as jnp
from jax import lax
from jax.experimental import pallas as pl
from jax.experimental.pallas import tpu as pltpu
from jax.sharding import PartitionSpec as P

MESH = pl.DeviceIdType.MESH
BF16 = jnp.bfloat16
F32 = jnp.float32
LOADS = 5
UPPER, MIXED, BACK, LOWER = range(4)
RIGHT, LEFT = range(2)


def torus(n_seq):
    return {128: (8, 4, 4), 8: (2, 2, 2)}[n_seq]


def dot(a, b, dims=((1,), (0,))):
    return lax.dot_general(a, b, (dims, ((), ())), preferred_element_type=F32)


def kernel(
    n_seq,
    x_hbm, g_hbm, y_hbm, r_hbm, l_hbm,
    ig_hbm, gg_hbm, rg_hbm, lg_hbm,
    xv, gv, yv, fac, out_s, out_r, part, spread, flat,
    bk, uk, lk,
    ig, gg, near_s, near_r, home_s, home_r, far_s, far_r, far_f, home_f, grad,
    load_sem, a2a_send, a2a_recv, sib_send, sib_recv, par_send, par_recv, fwd_send, fwd_recv,
    near_ss, near_rs, home_ss, home_rs, far_ss, far_rs, out_sem, row_sem, plane_sem,
):
    zs, ys, xs = torus(n_seq)
    blocks, order, width = fac.shape[1], fac.shape[2], xv.shape[1]
    quarter = order // 4
    dests = n_seq // 4
    piece = 4 * blocks
    seq, ch = lax.axis_index("seq"), lax.axis_index("chan")
    z, y, x = seq // (ys * xs), (seq // xs) % ys, seq % xs
    sib, par = ch ^ 1, ch ^ 2

    def rows(start, size):
        return pl.ds(pl.multiple_of(start, size), size)

    mine = rows(ch * quarter, quarter)
    loads = [
        pltpu.make_async_copy(src, dst, load_sem.at[n])
        for n, (src, dst) in enumerate((
            (y_hbm, yv), (g_hbm, gv), (x_hbm, xv),
            (r_hbm, fac.at[RIGHT, :, mine, :]), (l_hbm, fac.at[LEFT, :, mine, :]),
        ))
    ]
    for load in loads:
        load.start()

    def seq_of(a, b, c):
        return (a % zs) * (ys * xs) + (b % ys) * xs + c % xs

    x_peers = [seq_of(z, y, x + d) for d in range(1, xs)]
    y_peers = [seq_of(z, y + d, x) for d in range(1, ys)]
    z_peers = [seq_of(z + d, y, x) for d in range(1, zs)]
    barrier = pltpu.get_barrier_semaphore()
    for d in range(1, 4):
        pl.semaphore_signal(barrier, inc=1, device_id={"chan": ch ^ d}, device_id_type=MESH)
    for p in x_peers + y_peers + z_peers:
        pl.semaphore_signal(barrier, inc=1, device_id={"seq": p}, device_id_type=MESH)
    pl.semaphore_wait(barrier, 3 + xs + ys + zs - 3)
    for p in y_peers:
        pl.semaphore_signal(row_sem, inc=1, device_id={"seq": p}, device_id_type=MESH)

    def chan_copy(src, dst, ss, rs, to):
        return pltpu.make_async_remote_copy(
            src_ref=src, dst_ref=dst, send_sem=ss, recv_sem=rs, device_id={"chan": to}, device_id_type=MESH
        )

    def factor_copy(which, n, ss, rs, owner, to, src=None):
        place = fac.at[which, n, rows(owner * quarter, quarter), :]
        return chan_copy(place if src is None else src.at[n], place, ss.at[which, n], rs.at[which, n], to)

    def to_sib(which, src):
        return [factor_copy(which, n, sib_send, sib_recv, ch, sib, src) for n in range(blocks)]

    def to_par(which, src):
        return [factor_copy(which, n, par_send, par_recv, ch, par, src) for n in range(blocks)]

    def passed_on(which):
        return [factor_copy(which, n, fwd_send, fwd_recv, par, sib) for n in range(blocks)]

    r_par, r_sib, r_fwd = to_par(RIGHT, r_hbm), to_sib(RIGHT, r_hbm), passed_on(RIGHT)
    l_par, l_sib, l_fwd = to_par(LEFT, l_hbm), to_sib(LEFT, l_hbm), passed_on(LEFT)
    for c in r_par + r_sib:
        c.start()

    def scatter_rows(local, count, base=0):
        for d in range(4):
            spread[pl.ds(base * piece + 4 * local + d, count, stride=piece), :] = part[pl.ds(d, count, stride=4), :]

    def send_piece(which, p):
        pltpu.make_async_remote_copy(
            src_ref=out_s.at[which, rows(p * piece, piece), :],
            dst_ref=out_r.at[which, rows(seq * piece, piece), :],
            send_sem=a2a_send.at[which],
            recv_sem=a2a_recv.at[which],
            device_id={"seq": p},
            device_id_type=MESH,
        ).start()

    def keep_own(which):
        here = rows(seq * piece, piece)
        out_r[which, here, :] = out_s[which, here, :]

    def send_all(which):
        def step(t, carry):
            u = (t * 37) % n_seq
            send_piece(which, seq_of(z + u // (ys * xs), y + (u // xs) % ys, x + u % xs))
            return carry

        lax.fori_loop(1, n_seq, step, 0)
        keep_own(which)

    def send_quarter(which, q):
        def step(t, carry):
            u = (t * 13) % dests
            p = q * dests + (seq + u) % dests

            @pl.when(p != seq)
            def _():
                send_piece(which, p)

            return carry

        lax.fori_loop(0, dests, step, 0)

    def wait_bytes(ref, sem):
        pltpu.make_async_copy(ref, ref, sem).wait()

    def wait_pieces(which, sem):
        wait_bytes(out_s.at[which, pl.ds(0, (n_seq - 1) * piece), :], sem.at[which])

    loads[0].wait()
    loads[1].wait()
    for n in range(blocks):
        block = pl.ds(n * order, order)
        part[...] = yv[block, :].astype(F32) * gv[block, :].astype(F32)
        scatter_rows(n, n_seq)
    out_s[BACK] = spread[...].astype(BF16)
    pl.semaphore_wait(row_sem, ys - 1)
    for p in z_peers:
        pl.semaphore_signal(plane_sem, inc=1, device_id={"seq": p}, device_id_type=MESH)
    loads[2].wait()
    loads[3].wait()

    def upper_quarter(q):
        for n in range(blocks):
            part[pl.ds(0, quarter), :] = dot(fac[RIGHT, n, rows(q * quarter, quarter), :], xv[pl.ds(n * order, order), :])
            scatter_rows(n, dests)
        size = dests * piece
        out_s[UPPER, rows(q * size, size), :] = spread[pl.ds(0, size), :].astype(BF16)

    upper_quarter(ch)
    pl.semaphore_wait(plane_sem, zs - 1)
    send_all(BACK)
    send_quarter(UPPER, ch)
    for c in r_sib:
        c.wait_recv()
    upper_quarter(sib)
    send_quarter(UPPER, sib)
    for c, f in zip(r_par, r_fwd):
        c.wait_recv()
        f.start()
    for c in l_par + l_sib:
        c.start()
    upper_quarter(par)
    send_quarter(UPPER, par)
    for f in r_fwd:
        f.wait_recv()
    upper_quarter(ch ^ 3)
    send_quarter(UPPER, ch ^ 3)
    keep_own(UPPER)

    for c, f in zip(l_par, l_fwd):
        c.wait_recv()
        f.start()
    loads[4].wait()
    wait_pieces(BACK, a2a_recv)
    flat[...] = out_r[BACK].astype(F32)
    for c in l_sib + l_fwd:
        c.wait_recv()
    for n in range(blocks):
        column = flat[pl.ds(n, order, stride=4), :]
        bk[n] = column.astype(BF16)
        part[...] = dot(column.T.astype(BF16), fac[LEFT, n]).T
        scatter_rows(n, n_seq)
    out_s[LOWER] = spread[...].astype(BF16)
    send_all(LOWER)

    wait_pieces(UPPER, a2a_recv)
    flat[...] = out_r[UPPER].astype(F32)
    for n in range(blocks):
        uk[n] = flat[pl.ds(n, order, stride=4), :].astype(BF16)
        part[...] = dot(fac[LEFT, n], uk[n])
        scatter_rows(n, n_seq)
    out_s[MIXED] = spread[...].astype(BF16)
    send_all(MIXED)

    def near_copy(which, n):
        return chan_copy(near_s.at[which, n], near_r.at[which, n], near_ss.at[which, n], near_rs.at[which, n], sib)

    def home_copy(which, n):
        return chan_copy(home_s.at[which, n], home_r.at[which, n], home_ss.at[which, n], home_rs.at[which, n], sib)

    def far_copy(which, n):
        return chan_copy(far_s.at[which, n], far_r.at[which, n], far_ss.at[which, n], far_rs.at[which, n], par)

    def grad_terms(which, a, b):
        def term(n, q):
            return dot(a(n, rows(q * quarter, quarter)), b(n), ((1,), (1,)))

        for n in range(blocks):
            near_s[which, n] = term(n, ch ^ 3).astype(BF16)
            near_copy(which, n).start()
        for n in range(blocks):
            far_f[n] = term(n, par)
        for n in range(blocks):
            near_copy(which, n).wait_recv()
            far_s[which, n] = (far_f[n] + near_r[which, n].astype(F32)).astype(BF16)
            far_copy(which, n).start()
        for n in range(blocks):
            home_s[which, n] = term(n, sib).astype(BF16)
            home_copy(which, n).start()
        for n in range(blocks):
            home_f[which, n] = term(n, ch)

    def grad_total(which, dst):
        for n in range(blocks):
            home_copy(which, n).wait_recv()
            far_copy(which, n).wait_recv()
            total = home_f[which, n] + home_r[which, n].astype(F32) + far_r[which, n].astype(F32)
            grad[which, n] = total.astype(BF16)
        copy = pltpu.make_async_copy(grad.at[which], dst, out_sem.at[which])
        copy.start()
        return copy

    grad_terms(LEFT, lambda n, r: bk[n, r, :], lambda n: uk[n])

    wait_pieces(LOWER, a2a_recv)
    flat[...] = out_r[LOWER].astype(F32)
    for n in range(blocks):
        lk[n] = flat[pl.ds(n, order, stride=4), :].astype(BF16)
    grad_terms(RIGHT, lambda n, r: lk[n, r, :], lambda n: xv[pl.ds(n * order, order), :])
    for n in range(blocks):
        column = flat[pl.ds(n, order, stride=4), :]
        ig[pl.ds(n * order, order), :] = dot(column.T.astype(BF16), fac[RIGHT, n]).T.astype(BF16)
    ig_out = pltpu.make_async_copy(ig, ig_hbm, out_sem.at[2])
    ig_out.start()

    wait_pieces(MIXED, a2a_recv)
    flat[...] = out_r[MIXED].astype(F32)
    for n in range(blocks):
        block = pl.ds(n * order, order)
        gg[block, :] = (yv[block, :].astype(F32) * flat[pl.ds(n, order, stride=4), :]).astype(BF16)
    gg_out = pltpu.make_async_copy(gg, gg_hbm, out_sem.at[3])
    gg_out.start()

    lg_out = grad_total(LEFT, lg_hbm)
    rg_out = grad_total(RIGHT, rg_hbm)
    for which in range(4):
        wait_pieces(which, a2a_send)
    for c in r_par + r_sib + r_fwd + l_par + l_sib + l_fwd:
        c.wait_send()
    for which in range(2):
        for n in range(blocks):
            near_copy(which, n).wait_send()
            home_copy(which, n).wait_send()
            far_copy(which, n).wait_send()
    for c in (ig_out, gg_out, lg_out, rg_out):
        c.wait()


def shards(n_seq, inputs, gate, cotangent, right_factor, left_factor):
    tokens, width = inputs.shape
    blocks, quarter, order = right_factor.shape
    piece = 4 * blocks
    data = (tokens, width)
    exchange = (4, n_seq * piece, width)
    terms = (2, blocks, quarter, order)
    dma = pltpu.SemaphoreType.DMA
    per_block = dma((2, blocks))
    scratch = (
        [pltpu.VMEM(data, BF16)] * 3
        + [pltpu.VMEM((2, blocks, order, order), BF16)]
        + [pltpu.VMEM(exchange, BF16)] * 2
        + [pltpu.VMEM((order, width), F32), pltpu.VMEM(exchange[1:], F32), pltpu.VMEM(exchange[1:], F32)]
        + [pltpu.VMEM((blocks, order, width), BF16)] * 3
        + [pltpu.VMEM(data, BF16)] * 2
        + [pltpu.VMEM(terms, BF16)] * 6
        + [pltpu.VMEM(terms[1:], F32), pltpu.VMEM(terms, F32), pltpu.VMEM(terms, BF16)]
        + [dma((LOADS,)), dma((4,)), dma((4,))]
        + [per_block] * 6
        + [per_block] * 6
        + [dma((4,)), pltpu.SemaphoreType.REGULAR, pltpu.SemaphoreType.REGULAR]
    )
    anywhere = pl.BlockSpec(memory_space=pl.ANY)
    flops = 12 * blocks * order * order * width
    return pl.pallas_call(
        functools.partial(kernel, n_seq),
        out_shape=(
            jax.ShapeDtypeStruct(data, BF16),
            jax.ShapeDtypeStruct(data, BF16),
            jax.ShapeDtypeStruct(right_factor.shape, BF16),
            jax.ShapeDtypeStruct(left_factor.shape, BF16),
        ),
        in_specs=[anywhere] * 5,
        out_specs=(anywhere,) * 4,
        scratch_shapes=scratch,
        compiler_params=pltpu.CompilerParams(
            collective_id=0, has_side_effects=True, vmem_limit_bytes=48 * 2**20
        ),
        cost_estimate=pl.CostEstimate(flops=flops, bytes_accessed=9 * 2**19, transcendentals=0),
        name="monarch",
    )(inputs, gate, cotangent, right_factor, left_factor)


def solution(mesh):
    rows = P("seq", "chan")
    factor = P("seq", "chan", None)
    return jax.shard_map(
        functools.partial(shards, mesh.shape["seq"]),
        mesh=mesh,
        in_specs=(rows, rows, rows, factor, factor),
        out_specs=(rows, rows, factor, factor),
        check_vma=False,
    )
```

time: 254 us -> 114 us (0.45)
  blocking collectives: 140 us -> 0 us
  Pallas kernels: 0 us -> 104 us
  waiting for transfers between devices: 79.2 us -> 0 us
  between operations: 13.9 us -> 0.65 us
  matrix products: 11.4 us -> 0 us
    all_to_all x4 -> x0, blocking collectives: 140 us -> none  [the longest x1 41.9 us: shards(): lax.all_to_all(upper, 'seq', split_axis=1, concat_axis=0, tiled=True)]
    pallas_call x0 -> x1, Pallas kernels: none -> 104 us  [shards(): pl.pallas_call(functools.partial(kernel, n_seq), out_shape=(jax.ShapeDtyp...]
    all_gather x2 -> x0, waiting for transfers between devices: 45.2 us -> none  [the longest x1 41.8 us: shards(): lax.all_gather(right_factor, 'chan', axis=1, tiled=True)]
    reduce_scatter x2 -> x0, waiting for transfers between devices: 32.6 us -> none  [the longest x1 32.6 us: shards(): lax.psum_scatter(right_terms.astype(jnp.bfloat16), 'chan', scatter_dimens...]
    dot_general x6 -> x0, matrix products: 11.4 us -> none  [the longest x1 2.41 us: shards(): jnp.einsum('kmi,ikc->mkc', lax.all_gather(left_factor, 'chan', axis=1, ti...]
    unnamed x14, local copies, waits for them, and re-layouts: 2.19 us -> 8.37 us
    convert_element_type x6 -> x0, local copies, waits for them, and re-layouts: 5.19 us -> none  [the longest x1 2.04 us: shards(): input_grad = input_grad.astype(jnp.bfloat16)]
  transfers between devices with their start and end apart: 4 -> 0, of which waited for: 3 -> 0; matrix products, arithmetic and copies ran while one was open for 4% -> 0% of each run, Pallas kernels for 0% -> 0%
where the time goes in v1:
time: 114 us; the launch traced here: 113 us
  Pallas kernels  104 us (91%)
  local copies, waits for them, and re-layouts  8.37 us (7%)
    pallas_call x1, Pallas kernels, shards(): pl.pallas_call(functools.partial(kernel, n_seq), out_shape=(jax.ShapeDtyp...  104 us
    unnamed x14, local copies, waits for them, and re-layouts  8.37 us

profile of v1, /device:TPU:1, one launch (start us, length us, event | category | flops | bytes accessed | tf_op | source)
XLA Modules:
  0.0 113.1 jit_solution(15296747327272369646)
XLA Ops:
  0.6 0.0 copy-start
  0.6 1.0 copy-done
  1.7 0.0 copy-start.1
  1.7 1.0 copy-done.1
  2.7 0.0 copy-start.2
  2.7 1.0 copy-done.2
  3.8 0.0 copy-start.3
  3.8 1.0 copy-done.3
  4.8 0.0 copy-start.4
  4.8 1.0 copy-done.4
  5.8 104.1 %monarch.1 = (bf16[2048,128]{1,0:T(8,128)(2,1)S(1)}, bf16[2048,128]{1,0:T(8,128)(2,1)S(1)}, bf16[4,128,512]{2,1,0:T(8,128)(2,1)S(1)}, bf16[4,128,512]{2,1,0:T(8,128)(2,1)S(1)}) custom-call(bf16[2048,128]{1,0:T(8,128)(2,1)S(1)} %copy-done, bf16[2048,128]{1,0:T(8,128)(2,1)S(1)} %copy-done.1, bf16[2048,128]{1,0:T(8,128)(2,1)S(1)} %copy-done.2, ...), custom_call_target="tpu_custom_call" | custom-call | flops 1610612736 | bytes 4718592 | tf_op jit(solution)/shard_map/monarch/pallas_call | solution.py:308
  110.0 0.8 copy.13
  110.8 0.8 copy.14
  111.6 0.8 copy.15
  112.4 0.8 copy.16
Async XLA Ops:
  0.6 1.0 copy-start
  1.7 1.0 copy-start.1
  2.7 1.0 copy-start.2
  3.8 1.0 copy-start.3
  4.8 1.0 copy-start.4

commit v2 on v1

--- a/solution.py
+++ b/solution.py
@@ -39,7 +39,7 @@
     dests = n_seq // 4
     piece = 4 * blocks
     seq, ch = lax.axis_index("seq"), lax.axis_index("chan")
-    z, y, x = seq // (ys * xs), (seq // xs) % ys, seq % xs
+    z, y, x = seq // (ys * xs), (seq // xs) & (ys - 1), seq & (xs - 1)
     sib, par = ch ^ 1, ch ^ 2
 
     def rows(start, size):
@@ -57,7 +57,7 @@
         load.start()
 
     def seq_of(a, b, c):
-        return (a % zs) * (ys * xs) + (b % ys) * xs + c % xs
+        return (a & (zs - 1)) * (ys * xs) + (b & (ys - 1)) * xs + (c & (xs - 1))
 
     x_peers = [seq_of(z, y, x + d) for d in range(1, xs)]
     y_peers = [seq_of(z, y + d, x) for d in range(1, ys)]
@@ -114,8 +114,8 @@
 
     def send_all(which):
         def step(t, carry):
-            u = (t * 37) % n_seq
-            send_piece(which, seq_of(z + u // (ys * xs), y + (u // xs) % ys, x + u % xs))
+            u = (t * 37) & (n_seq - 1)
+            send_piece(which, seq_of(z + u // (ys * xs), y + u // xs, x + u))
             return carry
 
         lax.fori_loop(1, n_seq, step, 0)
@@ -123,8 +123,8 @@
 
     def send_quarter(which, q):
         def step(t, carry):
-            u = (t * 13) % dests
-            p = q * dests + (seq + u) % dests
+            u = (t * 13) & (dests - 1)
+            p = q * dests + ((seq + u) & (dests - 1))
 
             @pl.when(p != seq)
             def _():
@@ -277,6 +277,15 @@
             home_copy(which, n).wait_send()
             far_copy(which, n).wait_send()
     for c in (ig_out, gg_out, lg_out, rg_out):
+        c.wait()
+
+
+def hand_over(*refs):
+    sem = refs[-1]
+    copies = [pltpu.make_async_copy(refs[n], refs[4 + n], sem.at[n]) for n in range(4)]
+    for c in copies:
+        c.start()
+    for c in copies:
         c.wait()
 
 
@@ -303,9 +312,9 @@
         + [per_block] * 6
         + [dma((4,)), pltpu.SemaphoreType.REGULAR, pltpu.SemaphoreType.REGULAR]
     )
-    anywhere = pl.BlockSpec(memory_space=pl.ANY)
+    in_hbm = pl.BlockSpec(memory_space=pltpu.HBM)
     flops = 12 * blocks * order * order * width
-    return pl.pallas_call(
+    results = pl.pallas_call(
         functools.partial(kernel, n_seq),
         out_shape=(
             jax.ShapeDtypeStruct(data, BF16),
@@ -313,15 +322,23 @@
             jax.ShapeDtypeStruct(right_factor.shape, BF16),
             jax.ShapeDtypeStruct(left_factor.shape, BF16),
         ),
-        in_specs=[anywhere] * 5,
-        out_specs=(anywhere,) * 4,
+        in_specs=[in_hbm] * 5,
+        out_specs=(in_hbm,) * 4,
         scratch_shapes=scratch,
         compiler_params=pltpu.CompilerParams(
             collective_id=0, has_side_effects=True, vmem_limit_bytes=48 * 2**20
         ),
         cost_estimate=pl.CostEstimate(flops=flops, bytes_accessed=9 * 2**19, transcendentals=0),
         name="monarch",
-    )(inputs, gate, cotangent, right_factor, left_factor)
+    )(*(pltpu.with_memory_space_constraint(a, pltpu.HBM) for a in (inputs, gate, cotangent, right_factor, left_factor)))
+    return pl.pallas_call(
+        hand_over,
+        out_shape=tuple(jax.ShapeDtypeStruct(r.shape, r.dtype) for r in results),
+        in_specs=[in_hbm] * 4,
+        out_specs=(in_hbm,) * 4,
+        scratch_shapes=[dma((4,))],
+        name="hand_over",
+    )(*results)
 
 
 def solution(mesh):

time: 114 us -> 173 us (1.52)
  Pallas kernels: 104 us -> 168 us
  local copies, waits for them, and re-layouts: 8.37 us -> 3.18 us
    pallas_call x0 -> x1, Pallas kernels: none -> 64.7 us  [shards(): pl.pallas_call(hand_over, out_shape=tuple((jax.ShapeDtypeStruct(r.shape,...]
    unnamed x14 -> x8, local copies, waits for them, and re-layouts: 8.37 us -> 3.18 us
where the time goes in v2:
time: 173 us; the launch traced here: 172 us
  Pallas kernels  168 us (97%)
  local copies, waits for them, and re-layouts  3.18 us (2%)
    pallas_call x1, Pallas kernels, shards(): pl.pallas_call(functools.partial(kernel, n_seq), out_shape=(jax.ShapeDtyp...  104 us
    pallas_call x1, Pallas kernels, shards(): pl.pallas_call(hand_over, out_shape=tuple((jax.ShapeDtypeStruct(r.shape,...  64.7 us

profile of v2, /device:TPU:1, one launch (start us, length us, event | category | flops | bytes accessed | tf_op | source)
XLA Modules:
  0.0 172.3 jit_solution(10720031456898954283)
XLA Ops:
  0.6 103.8 %monarch.1 = (bf16[2048,128]{1,0:T(8,128)(2,1)S(1)}, bf16[2048,128]{1,0:T(8,128)(2,1)S(1)}, bf16[4,128,512]{2,1,0:T(8,128)(2,1)S(1)}, bf16[4,128,512]{2,1,0:T(8,128)(2,1)S(1)}) custom-call(bf16[2048,128]{1,0:T(8,128)(2,1)} %x_hbm.1, bf16[2048,128]{1,0:T(8,128)(2,1)} %g_hbm.1, bf16[2048,128]{1,0:T(8,128)(2,1)} %y_hbm.1, bf16[4,128,512]{2,1,0:T(8,128)(2,1)} %r_hbm.1, ...), custom_call_target="tpu_custom_call" | custom-call | flops 1610612736 | bytes 4718592 | tf_op jit(solution)/shard_map/monarch/pallas_call | solution.py:317
  104.5 0.0 copy-start
  104.5 0.8 copy-done
  105.3 0.0 copy-start.1
  105.3 0.8 copy-done.1
  106.1 0.0 copy-start.2
  106.1 0.8 copy-done.2
  106.9 0.0 copy-start.3
  106.9 0.8 copy-done.3
  107.7 64.7 %hand_over.1 = (bf16[2048,128]{1,0:T(8,128)(2,1)}, bf16[2048,128]{1,0:T(8,128)(2,1)}, bf16[4,128,512]{2,1,0:T(8,128)(2,1)}, bf16[4,128,512]{2,1,0:T(8,128)(2,1)}) custom-call(bf16[2048,128]{1,0:T(8,128)(2,1)} %copy-done, bf16[2048,128]{1,0:T(8,128)(2,1)} %copy-done.1, bf16[4,128,512]{2,1,0:T(8,128)(2,1)} %copy-done.2, bf16[4,128,512]{2,1,0:T(8,128)(2,1)} %copy-done.3), custom_call_target="tpu_custom_call" | custom-call | tf_op jit(solution)/shard_map/hand_over/pallas_call | solution.py:334
Async XLA Ops:
  104.5 0.8 copy-start
  105.3 0.8 copy-start.1
  106.1 0.8 copy-start.2
  106.9 0.8 copy-start.3

commit v3 on v2

v3 whole, which is shorter than its diff:
```python
import functools

import jax
import jax.numpy as jnp
from jax import lax
from jax.experimental import pallas as pl
from jax.experimental.pallas import tpu as pltpu
from jax.sharding import PartitionSpec as P

MESH = pl.DeviceIdType.MESH
BF16 = jnp.bfloat16
F32 = jnp.float32
UPPER, MIXED, BACK, LOWER = range(4)
RIGHT, LEFT = range(2)
OWN, SIB = range(2)


def torus(n_seq):
    return {128: (8, 4, 4), 8: (2, 2, 2)}[n_seq]


def dot(a, b, dims=((1,), (0,))):
    return lax.dot_general(a, b, (dims, ((), ())), preferred_element_type=F32)


def kernel(
    n_seq,
    x_hbm, g_hbm, y_hbm, r_hbm, l_hbm,
    ig_hbm, gg_hbm, rg_hbm, lg_hbm,
    xv, gv, yv, gated, right, left, out_s, out_r, sib_r, part, spread, flat,
    bk, uk, lk, ig, gg, far_s, far_r, far_l, home_f, grad,
    load_sem, a2a_send, a2a_recv, share_send, share_recv, in_send, in_recv,
    sib_send, sib_recv, par_send, par_recv, fwd_send, fwd_recv,
    far_ss, far_rs, out_sem, row_sem, plane_sem,
):
    zs, ys, xs = torus(n_seq)
    blocks, order, width = right.shape[0], right.shape[1], gv.shape[1]
    quarter = order // 4
    dests = n_seq // 4
    piece = 4 * blocks
    seq, ch = lax.axis_index("seq"), lax.axis_index("chan")
    z, y, x = seq // (ys * xs), (seq // xs) & (ys - 1), seq & (xs - 1)
    chip, core = ch // 2, ch & 1
    sib, par, twist = ch ^ 1, ch ^ 2, 2 * core + chip

    def rows(start, size):
        return pl.ds(pl.multiple_of(start, size), size)

    def lanes(r):
        return pl.ds(r * width, width)

    mine = rows(ch * quarter, quarter)
    loads = [
        pltpu.make_async_copy(src, dst, load_sem.at[n])
        for n, (src, dst) in enumerate((
            (y_hbm, yv), (g_hbm, gv), (r_hbm, right.at[:, mine, :]), (x_hbm, xv.at[:, lanes(OWN)]),
            (l_hbm.at[pl.ds(2 * chip, 2)], left.at[:, mine, :]),
        ))
    ]
    for load in loads:
        load.start()

    def seq_of(a, b, c):
        return (a & (zs - 1)) * (ys * xs) + (b & (ys - 1)) * xs + (c & (xs - 1))

    y_peers = [seq_of(z, y + d, x) for d in range(1, ys)]
    z_peers = [seq_of(z + d, y, x) for d in range(1, zs)]
    barrier = pltpu.get_barrier_semaphore()
    for d in range(1, 4):
        pl.semaphore_signal(barrier, inc=1, device_id={"chan": ch ^ d}, device_id_type=MESH)
    for p in y_peers + z_peers:
        pl.semaphore_signal(barrier, inc=1, device_id={"seq": p}, device_id_type=MESH)
    for d in range(1, xs):
        to = {"seq": seq_of(z, y, x + d), "chan": twist}
        pl.semaphore_signal(barrier, inc=1, device_id=to, device_id_type=MESH)
    pl.semaphore_wait(barrier, 3 + xs + ys + zs - 3)

    def chan_copy(src, dst, ss, rs, to):
        return pltpu.make_async_remote_copy(
            src_ref=src, dst_ref=dst, send_sem=ss, recv_sem=rs, device_id={"chan": to}, device_id_type=MESH
        )

    def right_copy(n, sems, owner, to, src=None):
        place = right.at[n, rows(owner * quarter, quarter), :]
        return chan_copy(place if src is None else src, place, sems[0].at[RIGHT, n], sems[1].at[RIGHT, n], to)

    def left_copy(n, sems, owner, to, src=None):
        place = left.at[n, rows(owner * quarter, quarter), :]
        return chan_copy(place if src is None else src, place, sems[0].at[LEFT, n], sems[1].at[LEFT, n], to)

    sib_sems, par_sems, fwd_sems = (sib_send, sib_recv), (par_send, par_recv), (fwd_send, fwd_recv)
    r_par = [right_copy(n, par_sems, ch, par, r_hbm.at[n]) for n in range(blocks)]
    r_sib = [right_copy(n, sib_sems, ch, sib, r_hbm.at[n]) for n in range(blocks)]
    r_fwd = [right_copy(n, fwd_sems, par, sib) for n in range(blocks)]
    l_par = [left_copy(n, par_sems, ch, par, l_hbm.at[2 * (1 - chip) + n]) for n in range(2)]
    l_sib = [left_copy(n, sib_sems, ch, sib, l_hbm.at[2 * chip + n]) for n in range(2)]
    l_fwd = [left_copy(n, fwd_sems, par, sib) for n in range(2)]
    x_sib = chan_copy(x_hbm, xv.at[:, lanes(SIB)], in_send.at[0], in_recv.at[0], sib)
    b_sib = chan_copy(gated.at[OWN], gated.at[SIB], in_send.at[1], in_recv.at[1], sib)
    for c in r_par + [x_sib] + r_sib:
        c.start()
    for p in y_peers:
        pl.semaphore_signal(row_sem, inc=1, device_id={"seq": p}, device_id_type=MESH)

    def to_piece(r, row, first, count):
        spread[pl.ds(row, count, stride=piece), :] = part[r, pl.ds(first, count, stride=4), :]

    def to_columns(r, local, count):
        for d in range(2):
            to_piece(r, 4 * local + 2 * d + r, 2 * core + d, count)

    def to_positions(r, d):
        for local in range(4):
            to_piece(r, 4 * (2 * d + r) + local, local, n_seq)

    def piece_copy(which, p):
        return pltpu.make_async_remote_copy(
            src_ref=out_s.at[which, rows(p * piece, piece), :],
            dst_ref=out_r.at[which, rows(seq * piece, piece), :],
            send_sem=a2a_send.at[which],
            recv_sem=a2a_recv.at[which],
            device_id={"seq": p, "chan": twist},
            device_id_type=MESH,
        )

    def send_own(which):
        @pl.when(chip == core)
        def _():
            here = rows(seq * piece, piece)
            out_r[which, here, :] = out_s[which, here, :]

        @pl.when(chip != core)
        def _():
            piece_copy(which, seq).start()

    def send_all(which):
        def step(t, carry):
            u = (t * 37) & (n_seq - 1)
            piece_copy(which, seq_of(z + u // (ys * xs), y + u // xs, x + u)).start()
            return carry

        lax.fori_loop(1, n_seq, step, 0)
        send_own(which)

    def send_quarter(which, q):
        def step(t, carry):
            u = (t * 13) & (dests - 1)
            p = q * dests + ((seq + u) & (dests - 1))

            @pl.when(p != seq)
            def _():
                piece_copy(which, p).start()

            return carry

        lax.fori_loop(0, dests, step, 0)

    def wait_pieces(which, sem):
        def wait_for(count):
            ref = out_s.at[which, pl.ds(0, count * piece), :]
            pltpu.make_async_copy(ref, ref, sem.at[which]).wait()

        pl.when(chip == core)(lambda: wait_for(n_seq - 1))
        pl.when(chip != core)(lambda: wait_for(n_seq))

    def share(which):
        return chan_copy(out_r.at[which], sib_r.at[which], share_send.at[which], share_recv.at[which], sib)

    def arrived(which):
        wait_pieces(which, a2a_recv)
        share(which).start()
        flat[OWN] = out_r[which].astype(F32)

    def shared(which):
        share(which).wait_recv()
        flat[SIB] = sib_r[which].astype(F32)

    loads[0].wait()
    loads[1].wait()
    for n in range(blocks):
        block = pl.ds(n * order, order)
        part[OWN] = yv[block, :].astype(F32) * gv[block, :].astype(F32)
        gated[OWN, block, :] = part[OWN].astype(BF16)
        to_columns(OWN, n, n_seq)
    b_sib.start()
    pl.semaphore_wait(row_sem, ys - 1)
    for p in z_peers:
        pl.semaphore_signal(plane_sem, inc=1, device_id={"seq": p}, device_id_type=MESH)
    b_sib.wait_recv()
    for n in range(blocks):
        part[SIB] = gated[SIB, pl.ds(n * order, order), :].astype(F32)
        to_columns(SIB, n, n_seq)
    out_s[BACK] = spread[...].astype(BF16)
    pl.semaphore_wait(plane_sem, zs - 1)
    send_all(BACK)

    def upper_quarter(q):
        here = pl.ds(0, quarter)
        for n in range(blocks):
            terms = dot(right[n, rows(q * quarter, quarter), :], xv[pl.ds(n * order, order), :])
            for r in range(2):
                part[r, here, :] = terms[:, r * width:(r + 1) * width]
                to_columns(r, n, dests)
        size = dests * piece
        out_s[UPPER, rows(q * size, size), :] = spread[pl.ds(0, size), :].astype(BF16)
        send_quarter(UPPER, q)

    loads[2].wait()
    loads[3].wait()
    x_sib.wait_recv()
    upper_quarter(ch)
    for c in r_sib:
        c.wait_recv()
    upper_quarter(sib)
    for c, f in zip(r_par, r_fwd):
        c.wait_recv()
        f.start()
    for c in l_par + l_sib:
        c.start()
    upper_quarter(par)
    for f in r_fwd:
        f.wait_recv()
    upper_quarter(ch ^ 3)
    send_own(UPPER)

    for c, f in zip(l_par, l_fwd):
        c.wait_recv()
        f.start()
    loads[4].wait()
    arrived(BACK)
    for c in l_sib + l_fwd:
        c.wait_recv()
    for d in range(2):
        column = [flat[OWN, pl.ds(2 * d + r, order, stride=4), :] for r in range(2)]
        for r in range(2):
            bk[d, :, lanes(r)] = column[r].astype(BF16)
        turned = jnp.concatenate([column[r].T for r in range(2)], axis=0).astype(BF16)
        terms = dot(turned, left[d])
        for r in range(2):
            part[r] = terms[r * width:(r + 1) * width].T
            to_positions(r, d)
    out_s[LOWER] = spread[...].astype(BF16)
    send_all(LOWER)

    arrived(UPPER)
    for d in range(2):
        for r in range(2):
            uk[d, :, lanes(r)] = flat[OWN, pl.ds(2 * d + r, order, stride=4), :].astype(BF16)
        terms = dot(left[d], uk[d, :, pl.ds(0, 2 * width)])
        for r in range(2):
            part[r] = terms[:, r * width:(r + 1) * width]
            to_positions(r, d)
    out_s[MIXED] = spread[...].astype(BF16)
    send_all(MIXED)

    for which, dst in ((BACK, bk), (UPPER, uk)):
        shared(which)
        for d in range(2):
            for r in range(2):
                dst[d, :, lanes(2 + r)] = flat[SIB, pl.ds(2 * d + r, order, stride=4), :].astype(BF16)

    def left_far(d):
        place = grad.at[LEFT, 2 * chip + d]
        return chan_copy(far_l.at[d], place, far_ss.at[LEFT, d], far_rs.at[LEFT, d], par)

    for d in range(2):
        far_l[d] = dot(bk[d, rows(par * quarter, quarter), :], uk[d], ((1,), (1,))).astype(BF16)
        left_far(d).start()
    for d in range(2):
        grad[LEFT, 2 * chip + d] = dot(bk[d, rows(ch * quarter, quarter), :], uk[d], ((1,), (1,))).astype(BF16)

    def right_far(n):
        return chan_copy(far_s.at[n], far_r.at[n], far_ss.at[RIGHT, n], far_rs.at[RIGHT, n], par)

    def right_terms(n, q):
        return dot(lk[n, rows(q * quarter, quarter), :], xv[pl.ds(n * order, order), :], ((1,), (1,)))

    arrived(LOWER)
    shared(LOWER)
    for n in range(blocks):
        for held in (OWN, SIB):
            for d in range(2):
                for r in range(2):
                    part[r, pl.ds(2 * (core ^ held) + d, n_seq, stride=4), :] = (
                        flat[held, pl.ds(4 * (2 * d + (r ^ held)) + n, n_seq, stride=piece), :]
                    )
        for r in range(2):
            lk[n, :, lanes(r)] = part[r].astype(BF16)
        far_s[n] = right_terms(n, par).astype(BF16)
        right_far(n).start()
    for n in range(blocks):
        turned = lk[n, :, lanes(OWN)].astype(F32).T.astype(BF16)
        ig[pl.ds(n * order, order), :] = dot(turned, right[n]).T.astype(BF16)
    ig_out = pltpu.make_async_copy(ig, ig_hbm, out_sem.at[2])
    ig_out.start()
    for n in range(blocks):
        home_f[n] = right_terms(n, ch)

    arrived(MIXED)
    shared(MIXED)
    for n in range(blocks):
        block = pl.ds(n * order, order)
        for held in (OWN, SIB):
            for d in range(2):
                part[0, pl.ds(2 * (core ^ held) + d, n_seq, stride=4), :] = (
                    flat[held, pl.ds(4 * (2 * d + held) + n, n_seq, stride=piece), :]
                )
        gg[block, :] = (yv[block, :].astype(F32) * part[0]).astype(BF16)
    gg_out = pltpu.make_async_copy(gg, gg_hbm, out_sem.at[3])
    gg_out.start()

    for d in range(2):
        left_far(d).wait_recv()
    lg_out = pltpu.make_async_copy(grad.at[LEFT], lg_hbm, out_sem.at[LEFT])
    lg_out.start()
    for n in range(blocks):
        right_far(n).wait_recv()
        grad[RIGHT, n] = (home_f[n] + far_r[n].astype(F32)).astype(BF16)
    rg_out = pltpu.make_async_copy(grad.at[RIGHT], rg_hbm, out_sem.at[RIGHT])
    rg_out.start()

    for which in range(4):
        wait_pieces(which, a2a_send)
        share(which).wait_send()
    for c in r_par + r_sib + r_fwd + l_par + l_sib + l_fwd + [x_sib, b_sib]:
        c.wait_send()
    for d in range(2):
        left_far(d).wait_send()
    for n in range(blocks):
        right_far(n).wait_send()
    for c in (ig_out, gg_out, lg_out, rg_out):
        c.wait()


def hand_over(*refs):
    sem = refs[-1]
    copies = [pltpu.make_async_copy(refs[n], refs[4 + n], sem.at[n]) for n in range(4)]
    for c in copies:
        c.start()
    for c in copies:
        c.wait()


def shards(n_seq, inputs, gate, cotangent, right_factor, left_factor):
    tokens, width = inputs.shape
    blocks, quarter, order = right_factor.shape
    piece = 4 * blocks
    data = (tokens, width)
    pieces = (n_seq * piece, width)
    terms = (blocks, quarter, order)
    dma = pltpu.SemaphoreType.DMA
    per_block = dma((2, blocks))
    scratch = (
        [pltpu.VMEM((tokens, 2 * width), BF16)]
        + [pltpu.VMEM(data, BF16)] * 2
        + [pltpu.VMEM((2,) + data, BF16)]
        + [pltpu.VMEM((blocks, order, order), BF16), pltpu.VMEM((2, order, order), BF16)]
        + [pltpu.VMEM((4,) + pieces, BF16)] * 3
        + [pltpu.VMEM((2, order, width), F32), pltpu.VMEM(pieces, F32), pltpu.VMEM((2,) + pieces, F32)]
        + [pltpu.VMEM((2, order, 4 * width), BF16)] * 2
        + [pltpu.VMEM((blocks, order, 2 * width), BF16)]
        + [pltpu.VMEM(data, BF16)] * 2
        + [pltpu.VMEM(terms, BF16)] * 2
        + [pltpu.VMEM((2, quarter, order), BF16), pltpu.VMEM(terms, F32), pltpu.VMEM((2,) + terms, BF16)]
        + [dma((5,))]
        + [dma((4,))] * 4
        + [dma((2,))] * 2
        + [per_block] * 6
        + [per_block] * 2
        + [dma((4,)), pltpu.SemaphoreType.REGULAR, pltpu.SemaphoreType.REGULAR]
    )
    in_hbm = pl.BlockSpec(memory_space=pltpu.HBM)

    given = (inputs, gate, cotangent, right_factor, left_factor)
    results = pl.pallas_call(
        functools.partial(kernel, n_seq),
        out_shape=(
            jax.ShapeDtypeStruct(data, BF16),
            jax.ShapeDtypeStruct(data, BF16),
            jax.ShapeDtypeStruct(right_factor.shape, BF16),
            jax.ShapeDtypeStruct(left_factor.shape, BF16),
        ),
        in_specs=[in_hbm] * 5,
        out_specs=(in_hbm,) * 4,
        scratch_shapes=scratch,
        compiler_params=pltpu.CompilerParams(
            collective_id=0, has_side_effects=True, vmem_limit_bytes=48 * 2**20
        ),
        cost_estimate=pl.CostEstimate(
            flops=12 * blocks * order * order * width, bytes_accessed=9 * 2**19, transcendentals=0
        ),
        name="monarch",
    )(*(pltpu.with_memory_space_constraint(a, pltpu.HBM) for a in given))
    return pl.pallas_call(
        hand_over,
        out_shape=tuple(jax.ShapeDtypeStruct(r.shape, r.dtype) for r in results),
        in_specs=[pl.BlockSpec(memory_space=pltpu.VMEM)] * 4,
        out_specs=(in_hbm,) * 4,
        scratch_shapes=[dma((4,))],
        name="hand_over",
    )(*results)


def solution(mesh):
    rows = P("seq", "chan")
    factor = P("seq", "chan", None)
    return jax.shard_map(
        functools.partial(shards, mesh.shape["seq"]),
        mesh=mesh,
        in_specs=(rows, rows, rows, factor, factor),
        out_specs=(rows, rows, factor, factor),
        check_vma=False,
    )
```

time: 173 us -> 100 us (0.58)
  Pallas kernels: 168 us -> 95.3 us
    pallas_call x1, Pallas kernels: 64.7 us -> 2.86 us  [shards(): pl.pallas_call(hand_over, out_shape=tuple((jax.ShapeDtypeStruct(r.shape,...]
    pallas_call x1, Pallas kernels: 104 us -> 92.5 us  [shards(): pl.pallas_call(functools.partial(kernel, n_seq), out_shape=(jax.ShapeDtyp...]
where the time goes in v3:
time: 100 us; the launch traced here: 99.2 us
  Pallas kernels  95.3 us (95%)
  local copies, waits for them, and re-layouts  3.18 us (3%)
    pallas_call x1, Pallas kernels, shards(): pl.pallas_call(functools.partial(kernel, n_seq), out_shape=(jax.ShapeDtyp...  92.5 us
    unnamed x8, local copies, waits for them, and re-layouts  3.18 us
    pallas_call x1, Pallas kernels, shards(): pl.pallas_call(hand_over, out_shape=tuple((jax.ShapeDtypeStruct(r.shape,...  2.86 us

profile of v3, /device:TPU:1, one launch (start us, length us, event | category | flops | bytes accessed | tf_op | source)
XLA Modules:
  0.0 99.2 jit_solution(4057625281165956196)
XLA Ops:
  0.6 92.5 %monarch.1 = (bf16[2048,128]{1,0:T(8,128)(2,1)S(1)}, bf16[2048,128]{1,0:T(8,128)(2,1)S(1)}, bf16[4,128,512]{2,1,0:T(8,128)(2,1)S(1)}, bf16[4,128,512]{2,1,0:T(8,128)(2,1)S(1)}) custom-call(bf16[2048,128]{1,0:T(8,128)(2,1)} %x_hbm.1, bf16[2048,128]{1,0:T(8,128)(2,1)} %g_hbm.1, bf16[2048,128]{1,0:T(8,128)(2,1)} %y_hbm.1, bf16[4,128,512]{2,1,0:T(8,128)(2,1)} %r_hbm.1, ...), custom_call_target="tpu_custom_call" | custom-call | flops 1610612736 | bytes 4718592 | tf_op jit(solution)/shard_map/monarch/pallas_call | solution.py:375
  93.1 0.0 copy-start
  93.1 0.8 copy-done
  93.9 0.0 copy-start.1
  93.9 0.8 copy-done.1
  94.7 0.0 copy-start.2
  94.7 0.8 copy-done.2
  95.5 0.0 copy-start.3
  95.5 0.8 copy-done.3
  96.3 2.9 %hand_over.1 = (bf16[2048,128]{1,0:T(8,128)(2,1)}, bf16[2048,128]{1,0:T(8,128)(2,1)}, bf16[4,128,512]{2,1,0:T(8,128)(2,1)}, bf16[4,128,512]{2,1,0:T(8,128)(2,1)}) custom-call(bf16[2048,128]{1,0:T(8,128)(2,1)} %copy-done, bf16[2048,128]{1,0:T(8,128)(2,1)} %copy-done.1, bf16[4,128,512]{2,1,0:T(8,128)(2,1)} %copy-done.2, bf16[4,128,512]{2,1,0:T(8,128)(2,1)} %copy-done.3), custom_call_target="tpu_custom_call" | custom-call | tf_op jit(solution)/shard_map/hand_over/pallas_call | solution.py:394
Async XLA Ops:
  93.1 0.8 copy-start
  93.9 0.8 copy-start.1
  94.7 0.8 copy-start.2
  95.5 0.8 copy-start.3

commit v4 on v3

--- a/solution.py
+++ b/solution.py
@@ -97,7 +97,7 @@
     l_fwd = [left_copy(n, fwd_sems, par, sib) for n in range(2)]
     x_sib = chan_copy(x_hbm, xv.at[:, lanes(SIB)], in_send.at[0], in_recv.at[0], sib)
     b_sib = chan_copy(gated.at[OWN], gated.at[SIB], in_send.at[1], in_recv.at[1], sib)
-    for c in r_par + [x_sib] + r_sib:
+    for c in r_par + l_par + [x_sib] + r_sib + l_sib:
         c.start()
     for p in y_peers:
         pl.semaphore_signal(row_sem, inc=1, device_id={"seq": p}, device_id_type=MESH)
@@ -174,6 +174,12 @@
     def shared(which):
         share(which).wait_recv()
         flat[SIB] = sib_r[which].astype(F32)
+
+    outs = []
+
+    def put(src, dst, place, which, n):
+        outs.append(pltpu.make_async_copy(src.at[place], dst.at[place], out_sem.at[which, n]))
+        outs[-1].start()
 
     loads[0].wait()
     loads[1].wait()
@@ -215,8 +221,6 @@
     for c, f in zip(r_par, r_fwd):
         c.wait_recv()
         f.start()
-    for c in l_par + l_sib:
-        c.start()
     upper_quarter(par)
     for f in r_fwd:
         f.wait_recv()
@@ -266,8 +270,6 @@
     for d in range(2):
         far_l[d] = dot(bk[d, rows(par * quarter, quarter), :], uk[d], ((1,), (1,))).astype(BF16)
         left_far(d).start()
-    for d in range(2):
-        grad[LEFT, 2 * chip + d] = dot(bk[d, rows(ch * quarter, quarter), :], uk[d], ((1,), (1,))).astype(BF16)
 
     def right_far(n):
         return chan_copy(far_s.at[n], far_r.at[n], far_ss.at[RIGHT, n], far_rs.at[RIGHT, n], par)
@@ -291,10 +293,12 @@
     for n in range(blocks):
         turned = lk[n, :, lanes(OWN)].astype(F32).T.astype(BF16)
         ig[pl.ds(n * order, order), :] = dot(turned, right[n]).T.astype(BF16)
-    ig_out = pltpu.make_async_copy(ig, ig_hbm, out_sem.at[2])
-    ig_out.start()
+        put(ig, ig_hbm, pl.ds(n * order, order), 2, n)
     for n in range(blocks):
         home_f[n] = right_terms(n, ch)
+    for d in range(2):
+        grad[LEFT, 2 * chip + d] = dot(bk[d, rows(ch * quarter, quarter), :], uk[d], ((1,), (1,))).astype(BF16)
+        put(grad.at[LEFT], lg_hbm, 2 * chip + d, LEFT, d)
 
     arrived(MIXED)
     shared(MIXED)
@@ -306,18 +310,15 @@
                     flat[held, pl.ds(4 * (2 * d + held) + n, n_seq, stride=piece), :]
                 )
         gg[block, :] = (yv[block, :].astype(F32) * part[0]).astype(BF16)
-    gg_out = pltpu.make_async_copy(gg, gg_hbm, out_sem.at[3])
-    gg_out.start()
+        put(gg, gg_hbm, block, 3, n)
 
     for d in range(2):
         left_far(d).wait_recv()
-    lg_out = pltpu.make_async_copy(grad.at[LEFT], lg_hbm, out_sem.at[LEFT])
-    lg_out.start()
+        put(grad.at[LEFT], lg_hbm, 2 * (1 - chip) + d, LEFT, 2 + d)
     for n in range(blocks):
         right_far(n).wait_recv()
         grad[RIGHT, n] = (home_f[n] + far_r[n].astype(F32)).astype(BF16)
-    rg_out = pltpu.make_async_copy(grad.at[RIGHT], rg_hbm, out_sem.at[RIGHT])
-    rg_out.start()
+        put(grad.at[RIGHT], rg_hbm, n, RIGHT, n)
 
     for which in range(4):
         wait_pieces(which, a2a_send)
@@ -328,7 +329,7 @@
         left_far(d).wait_send()
     for n in range(blocks):
         right_far(n).wait_send()
-    for c in (ig_out, gg_out, lg_out, rg_out):
+    for c in outs:
         c.wait()
 
 
@@ -367,7 +368,7 @@
         + [dma((2,))] * 2
         + [per_block] * 6
         + [per_block] * 2
-        + [dma((4,)), pltpu.SemaphoreType.REGULAR, pltpu.SemaphoreType.REGULAR]
+        + [dma((4, blocks)), pltpu.SemaphoreType.REGULAR, pltpu.SemaphoreType.REGULAR]
     )
     in_hbm = pl.BlockSpec(memory_space=pltpu.HBM)
 
@@ -397,6 +398,7 @@
         in_specs=[pl.BlockSpec(memory_space=pltpu.VMEM)] * 4,
         out_specs=(in_hbm,) * 4,
         scratch_shapes=[dma((4,))],
+        compiler_params=pltpu.CompilerParams(vmem_limit_bytes=2**20),
         name="hand_over",
     )(*results)
 

time: 100 us -> 95.6 us (0.956)
  local copies, waits for them, and re-layouts: 3.18 us -> 0 us
    unnamed x8 -> x0, local copies, waits for them, and re-layouts: 3.18 us -> none
    pallas_call x1, Pallas kernels: 2.86 us -> 1.35 us  [shards(): pl.pallas_call(hand_over, out_shape=tuple((jax.ShapeDtypeStruct(r.shape,...]
where the time goes in v4:
time: 95.6 us; the launch traced here: 95.4 us
  Pallas kernels  94.8 us (99%)
    pallas_call x1, Pallas kernels, shards(): pl.pallas_call(functools.partial(kernel, n_seq), out_shape=(jax.ShapeDtyp...  93.4 us

profile of v4, /device:TPU:1, one launch (start us, length us, event | category | flops | bytes accessed | tf_op | source)
XLA Modules:
  0.0 95.4 jit_solution(3188176652555720025)
XLA Ops:
  0.6 93.4 %monarch.1 = (bf16[2048,128]{1,0:T(8,128)(2,1)S(1)}, bf16[2048,128]{1,0:T(8,128)(2,1)S(1)}, bf16[4,128,512]{2,1,0:T(8,128)(2,1)S(1)}, bf16[4,128,512]{2,1,0:T(8,128)(2,1)S(1)}) custom-call(bf16[2048,128]{1,0:T(8,128)(2,1)} %x_hbm.1, bf16[2048,128]{1,0:T(8,128)(2,1)} %g_hbm.1, bf16[2048,128]{1,0:T(8,128)(2,1)} %y_hbm.1, bf16[4,128,512]{2,1,0:T(8,128)(2,1)} %r_hbm.1, ...), custom_call_target="tpu_custom_call" | custom-call | flops 1610612736 | bytes 4718592 | tf_op jit(solution)/shard_map/monarch/pallas_call | solution.py:376
  94.1 1.3 %hand_over.1 = (bf16[2048,128]{1,0:T(8,128)(2,1)}, bf16[2048,128]{1,0:T(8,128)(2,1)}, bf16[4,128,512]{2,1,0:T(8,128)(2,1)}, bf16[4,128,512]{2,1,0:T(8,128)(2,1)}) custom-call(bf16[2048,128]{1,0:T(8,128)(2,1)S(1)} %get-tuple-element.8.refs_0_, bf16[2048,128]{1,0:T(8,128)(2,1)S(1)} %get-tuple-element.9.refs_1_, ...), custom_call_target="tpu_custom_call" | custom-call | tf_op jit(solution)/shard_map/hand_over/pallas_call | solution.py:395

commit v5 on v4

--- a/solution.py
+++ b/solution.py
@@ -135,11 +135,15 @@
 
     def send_all(which):
         def step(t, carry):
-            u = (t * 37) & (n_seq - 1)
-            piece_copy(which, seq_of(z + u // (ys * xs), y + u // xs, x + u)).start()
+            p = (t * 37) & (n_seq - 1)
+
+            @pl.when(p != seq)
+            def _():
+                piece_copy(which, p).start()
+
             return carry
 
-        lax.fori_loop(1, n_seq, step, 0)
+        lax.fori_loop(0, n_seq, step, 0)
         send_own(which)
 
     def send_quarter(which, q):
@@ -166,9 +170,11 @@
     def share(which):
         return chan_copy(out_r.at[which], sib_r.at[which], share_send.at[which], share_recv.at[which], sib)
 
-    def arrived(which):
+    def arrived(which, held_back=()):
         wait_pieces(which, a2a_recv)
         share(which).start()
+        for c in held_back:
+            c.start()
         flat[OWN] = out_r[which].astype(F32)
 
     def shared(which):
@@ -269,7 +275,8 @@
 
     for d in range(2):
         far_l[d] = dot(bk[d, rows(par * quarter, quarter), :], uk[d], ((1,), (1,))).astype(BF16)
-        left_far(d).start()
+        if d < 1:
+            left_far(d).start()
 
     def right_far(n):
         return chan_copy(far_s.at[n], far_r.at[n], far_ss.at[RIGHT, n], far_rs.at[RIGHT, n], par)
@@ -277,7 +284,7 @@
     def right_terms(n, q):
         return dot(lk[n, rows(q * quarter, quarter), :], xv[pl.ds(n * order, order), :], ((1,), (1,)))
 
-    arrived(LOWER)
+    arrived(LOWER, [left_far(1)])
     shared(LOWER)
     for n in range(blocks):
         for held in (OWN, SIB):

time: 95.6 us -> 94.8 us (level)
  no operation moved by 1% of the time
where the time goes in v5:
time: 94.8 us; the launch traced here: 94.7 us
  Pallas kernels  94.1 us (99%)
    pallas_call x1, Pallas kernels, shards(): pl.pallas_call(functools.partial(kernel, n_seq), out_shape=(jax.ShapeDtyp...  92.7 us

profile of v5, /device:TPU:1, one launch (start us, length us, event | category | flops | bytes accessed | tf_op | source)
XLA Modules:
  0.0 94.7 jit_solution(9828400909869462516)
XLA Ops:
  0.6 92.7 %monarch.1 = (bf16[2048,128]{1,0:T(8,128)(2,1)S(1)}, bf16[2048,128]{1,0:T(8,128)(2,1)S(1)}, bf16[4,128,512]{2,1,0:T(8,128)(2,1)S(1)}, bf16[4,128,512]{2,1,0:T(8,128)(2,1)S(1)}) custom-call(bf16[2048,128]{1,0:T(8,128)(2,1)} %x_hbm.1, bf16[2048,128]{1,0:T(8,128)(2,1)} %g_hbm.1, bf16[2048,128]{1,0:T(8,128)(2,1)} %y_hbm.1, bf16[4,128,512]{2,1,0:T(8,128)(2,1)} %r_hbm.1, ...), custom_call_target="tpu_custom_call" | custom-call | flops 1610612736 | bytes 4718592 | tf_op jit(solution)/shard_map/monarch/pallas_call | solution.py:383
  93.4 1.3 %hand_over.1 = (bf16[2048,128]{1,0:T(8,128)(2,1)}, bf16[2048,128]{1,0:T(8,128)(2,1)}, bf16[4,128,512]{2,1,0:T(8,128)(2,1)}, bf16[4,128,512]{2,1,0:T(8,128)(2,1)}) custom-call(bf16[2048,128]{1,0:T(8,128)(2,1)S(1)} %get-tuple-element.8.refs_0_, bf16[2048,128]{1,0:T(8,128)(2,1)S(1)} %get-tuple-element.9.refs_1_, ...), custom_call_target="tpu_custom_call" | custom-call | tf_op jit(solution)/shard_map/hand_over/pallas_call | solution.py:402
